TPU v7x, 32 devices: a whole 2x2x4 slice. The times are simulated.
32 devices in a mesh: groups: 1, col: 16 (over z, y, x), facet: 1, pol: 2 (over core).
Axes of the slice: x: 2, y: 2, z: 4, core: 2. Of those that a mesh axis runs over, the one named last changes fastest.
Arguments:
- facets: float32 [16, 2, 8, 4096], P(('groups', 'col'), 'pol', 'facet'), may hold values from -6 to 6
- facet_offsets: int32 [16], P(('groups', 'col')), may hold values from 0 to 65535
- subgrid_offsets: int32 [16], P('groups'), may hold values from 0 to 65535
- row_counts: int32 [16], P(('groups', 'col', 'facet')), may hold values from 1536 to 2048, as said below
- dest_column: int32 [32768], P(('groups', 'col', 'facet')), may hold values from 0 to 15, as said below
- grid_row: int32 [32768], P(('groups', 'col', 'facet')), may hold values from 0 to 7
- position: float32 [32768], P(('groups', 'col', 'facet')), may hold values from 4 to 123
- observed: float32 [2, 2, 32768], P('pol', None, ('groups', 'col', 'facet')), may hold values from -6 to 6
Outputs:
- column_grid: float32 [16, 2, 8, 256], P(('groups', 'col'), 'pol', 'facet')
- residual: float32 [2, 2, 32768], P('pol', None, ('groups', 'col', 'facet'))
Inputs may be any that keep to these rules, and one draw needn't show every extreme that they name: The live rows of each shard are its first row_counts rows; some shard has all 2048 rows live. `dest_column`: among the live rows of one shard no column is named more than 256 times; for each facet index, some column is named exactly 256 times by the live rows of every shard with that facet index.
All inputs are finite; a program needn't handle non-finite values.
Results may differ from a plain program's by a relative error of at most 0.0037.
Values sent between devices are 32-bit elements; how exact they have to be, the bound alone decides.
A program may use at most 64 MiB of HBM per device.

v0:
```python
import math

import jax
import jax.numpy as jnp
from jax import lax
from jax.sharding import PartitionSpec as P

NIMG = 65536
M = 128
S = 8


TWO_PI = 2.0 * math.pi


def from_behind(array, axis, by):
    peers = lax.axis_size(axis)
    return lax.ppermute(array, axis, [(i, (i + by) % peers) for i in range(peers)])


def product_mod(left_value, right_value, modulus):
    upper_part = left_value // 256 * right_value % modulus
    return (upper_part * 256 + left_value % 256 * right_value) % modulus


def taper_values(pixels):
    places = jnp.arange(pixels, dtype=jnp.int32).astype(jnp.float32)
    offset = (2.0 * places + 1.0) / pixels - 1.0
    squared = 1.0 - offset * offset
    return squared * squared


def phase_table(pixels, frequency_count):
    places = jnp.arange(pixels, dtype=jnp.int32)[:, None]
    frequency = jnp.arange(frequency_count, dtype=jnp.int32)[None, :]
    angles = (places * frequency % NIMG).astype(jnp.float32) * (TWO_PI / NIMG)
    return jnp.concatenate([jnp.cos(angles), -jnp.sin(angles)], axis=1).astype(jnp.bfloat16)


def column_term(scaled, dft_table, column_offset, facet_offset):
    pixels = scaled.shape[1]
    row_total = scaled.shape[0]
    frequency_count = dft_table.shape[1] // 2
    places = jnp.arange(pixels, dtype=jnp.int32)
    angles = (places * column_offset % NIMG).astype(jnp.float32) * (TWO_PI / NIMG)
    trig_rows = jnp.stack([jnp.cos(angles), -jnp.sin(angles)])
    modulated = (
        (trig_rows[:, None, :] * scaled[None]).astype(jnp.bfloat16).reshape(2 * row_total, pixels)
    )
    product = jnp.dot(modulated, dft_table, preferred_element_type=jnp.float32)
    real_part = product[:row_total, :frequency_count] - product[row_total:, frequency_count:]
    imag_part = product[:row_total, frequency_count:] + product[row_total:, :frequency_count]
    frequency = jnp.arange(frequency_count, dtype=jnp.int32)
    turn_index = product_mod(facet_offset, (column_offset + frequency) % NIMG, NIMG)
    rotation = turn_index.astype(jnp.float32) * (TWO_PI / NIMG)
    norm_factor = 1.0 / math.sqrt(NIMG)
    cos_turn = jnp.cos(rotation) * norm_factor
    sin_turn = -jnp.sin(rotation) * norm_factor
    return jnp.concatenate(
        [real_part * cos_turn - imag_part * sin_turn, real_part * sin_turn + imag_part * cos_turn],
        axis=1,
    )


def body(
    facets, facet_offsets, subgrid_offsets, row_counts, dest_column, grid_row, position, observed
):
    owners = lax.axis_size("col")
    own_index = lax.axis_index("col")
    raw_rows = facets[0, 0]
    row_total = raw_rows.shape[0]
    window = taper_values(raw_rows.shape[1])
    facet_rows = raw_rows * window
    dft_table = phase_table(raw_rows.shape[1], M)
    own_offset = facet_offsets[0]

    def term_for(some_rows, column):
        return column_term(some_rows, dft_table, subgrid_offsets[column], own_offset)

    def cycle_step(kernel_step, partial_value):
        partial_value = partial_value + term_for(facet_rows, (own_index - 1 - kernel_step) % owners)
        return from_behind(partial_value, "col", 1)

    partial_value = lax.fori_loop(
        0, owners - 1, cycle_step, jnp.zeros((row_total, 2 * M), jnp.float32)
    )
    column_sum = partial_value + term_for(facet_rows, own_index)
    total_rows = dest_column.shape[0]
    capacity = 2 * total_rows // owners
    places = jnp.arange(total_rows, dtype=jnp.int32)
    live_rows = places < row_counts[0]
    one_hot = (
        (dest_column[:, None] == jnp.arange(owners, dtype=jnp.int32)[None, :]) & live_rows[:, None]
    ).astype(jnp.int32)
    earlier = jnp.cumsum(one_hot, axis=0) - one_hot
    rank_within = jnp.sum(earlier * one_hot, axis=1)
    slot_index = jnp.where(live_rows, dest_column * capacity + rank_within, owners * capacity)
    payload = jnp.stack([observed[0, 0], observed[0, 1], position])
    outgoing = (
        jnp.zeros((payload.shape[0], owners * capacity), jnp.float32)
        .at[:, slot_index]
        .set(payload, mode="drop")
    )
    outgoing = outgoing.reshape(payload.shape[0], owners, capacity)
    targets = (
        jnp.full((1, owners * capacity), -1, jnp.int32)
        .at[:, slot_index]
        .set(grid_row[None], mode="drop")
    )
    targets = targets.reshape(1, owners, capacity)
    flat_grid = column_sum.reshape(-1)
    floats = lax.all_to_all(outgoing, "col", split_axis=1, concat_axis=1, tiled=True)
    int_part = lax.all_to_all(targets, "col", split_axis=1, concat_axis=1, tiled=True)
    target = int_part[0]
    filled = target >= 0
    row_start = jnp.maximum(target, 0) * (2 * M)
    location = floats[-1]
    base_cell = jnp.floor(location).astype(jnp.int32) - S // 2 + 1
    real_sum = jnp.zeros(location.shape, jnp.float32)
    imag_sum = jnp.zeros(location.shape, jnp.float32)
    for kernel_step in range(S):
        cell_index = base_cell + kernel_step
        clipped = jnp.clip(cell_index, 0, M - 1)
        distance = cell_index.astype(jnp.float32) - location
        scaled_dist = 2.0 * distance / S
        weight = (1.0 - scaled_dist * scaled_dist) * (1.0 - scaled_dist * scaled_dist)
        real_sum = real_sum + weight * jnp.take(flat_grid, row_start + clipped)
        imag_sum = imag_sum + weight * jnp.take(flat_grid, row_start + M + clipped)
    answer = jnp.stack(
        [jnp.where(filled, floats[0] - real_sum, 0.0), jnp.where(filled, floats[1] - imag_sum, 0.0)]
    )
    returned = lax.all_to_all(answer, "col", split_axis=1, concat_axis=1, tiled=True)
    returned = returned.reshape(2, owners * capacity)
    picked = jnp.take(returned, jnp.minimum(slot_index, owners * capacity - 1), axis=1)
    residual = jnp.where(live_rows[None, :], picked, 0.0)
    return (column_sum.reshape(1, 1, row_total, 2 * M), residual[None])


def solution(mesh):
    placed = (
        P(("groups", "col"), "pol", "facet", None),
        P(("groups", "col")),
        P("groups"),
        P(("groups", "col", "facet")),
        P(("groups", "col", "facet")),
        P(("groups", "col", "facet")),
        P(("groups", "col", "facet")),
        P("pol", None, ("groups", "col", "facet")),
    )
    return jax.shard_map(
        body,
        mesh=mesh,
        in_specs=placed,
        out_specs=(
            P(("groups", "col"), "pol", "facet", None),
            P("pol", None, ("groups", "col", "facet")),
        ),
        check_vma=False,
    )
```

profile of v0, /device:TPU:0, one launch (start us, length us, event | category | flops | bytes accessed | tf_op | source)
XLA Modules:
  0.0 599.1 jit_solution(10276360785901171564)
XLA Ops:
  18.1 8.3 %all-to-all-start.1 = ((f32[3,16,256]{2,0,1:T(4,128)}), f32[3,16,256]{2,0,1:T(4,128)S(1)}, u32[]{:S(2)}, u32[]{:S(2)}) async-start(f32[3,16,256]{2,0,1:T(4,128)} %copy.20), calls=%async_computation.1 | async-start | bytes 131072 | tf_op jit(solution)/shard_map/all_to_all | solution.py:112
  27.1 9.2 %negate_convert_fusion = (bf16[4096,128]{1,0:T(8,128)(2,1)S(1)}, bf16[4096,128]{1,0:T(8,128)(2,1)}) fusion(), kind=kLoop, calls=%fused_computation.63 | loop fusion | flops 8912896 | bytes 2097152 | tf_op jit(solution)/shard_map/convert.1
  40.7 150.7 %while.17 = (s32[]{:T(128)}, f32[8,256]{1,0:T(8,128)S(1)}, s32[]{:T(128)}, s32[16]{0:T(128)S(1)}, f32[8,4096]{1,0:T(8,128)S(1)}, /*index=5*/bf16[4096,256]{1,0:T...) while((s32[]{:T(128)}, f32[8,256]{1,0:T(8,128)S(1)}, ...), condition=%wide.region_1.2_spmd, body=%wide.region_0.1_spmd.sunk | while | flops 33772944 | bytes 2459988 | solution.py:84
  53.6 7.2 %collective-permute-done = f32[8,256]{1,0:T(8,128)S(1)} collective-permute-done((f32[8,256]{1,0:T(8,128)S(1)}, f32[8,256]{1,0:T(8,128)S(1)}, u32[]{:S(2)}, u32[]{:S(2)}) %collective-permute-start) | collective-permute-done | bytes 8224 | tf_op jit(solution)/shard_map/while/body/eval_jaxpr/ppermute | solution.py:18
  63.6 7.2 %collective-permute-done = f32[8,256]{1,0:T(8,128)S(1)} collective-permute-done((f32[8,256]{1,0:T(8,128)S(1)}, f32[8,256]{1,0:T(8,128)S(1)}, u32[]{:S(2)}, u32[]{:S(2)}) %collective-permute-start) | collective-permute-done | bytes 8224 | tf_op jit(solution)/shard_map/while/body/eval_jaxpr/ppermute | solution.py:18
  73.7 7.2 %collective-permute-done = f32[8,256]{1,0:T(8,128)S(1)} collective-permute-done((f32[8,256]{1,0:T(8,128)S(1)}, f32[8,256]{1,0:T(8,128)S(1)}, u32[]{:S(2)}, u32[]{:S(2)}) %collective-permute-start) | collective-permute-done | bytes 8224 | tf_op jit(solution)/shard_map/while/body/eval_jaxpr/ppermute | solution.py:18
  192.0 8.8 %scatter_custom_fusion = s32[4096]{0:T(1024)} fusion(s32[2048]{0:T(1024)S(1)} %get-tuple-element.429, s32[2048]{0:T(1024)} %param.17, s32[]{:T(128)} %constant.326.clone.1), kind=kCustom, calls=%fused_computation.224 | custom fusion | bytes 16896 | tf_op jit(solution)/shard_map/scatter | solution.py:108
  211.7 23.0 %gather_fusion.1 = f32[4096]{0:T(1024)S(1)} fusion(f32[2048]{0:T(1024)S(1)} %bitcast.281, s32[4096]{0:T(1024)S(1)} %broadcast_clamp_fusion.15), kind=kCustom, calls=%fused_computation.clone | custom fusion | bytes 49152 | tf_op jit(solution)/shard_map/jit(_take)/gather | solution.py:127
  234.8 23.0 %gather_fusion.2 = f32[4096]{0:T(1024)S(1)} fusion(f32[2048]{0:T(1024)S(1)} %bitcast.282, s32[4096]{0:T(1024)S(1)} %broadcast_clamp_fusion.14), kind=kCustom, calls=%fused_computation.1.clone | custom fusion | bytes 49152 | tf_op jit(solution)/shard_map/jit(_take)/gather | solution.py:127
  257.8 23.0 %gather_fusion.3 = f32[4096]{0:T(1024)S(1)} fusion(f32[2048]{0:T(1024)S(1)} %bitcast.283, s32[4096]{0:T(1024)S(1)} %broadcast_clamp_fusion.13), kind=kCustom, calls=%fused_computation.2.clone | custom fusion | bytes 49152 | tf_op jit(solution)/shard_map/jit(_take)/gather | solution.py:127
  280.9 23.0 %gather_fusion.4 = f32[4096]{0:T(1024)S(1)} fusion(f32[2048]{0:T(1024)S(1)} %bitcast.284, s32[4096]{0:T(1024)S(1)} %broadcast_clamp_fusion.12), kind=kCustom, calls=%fused_computation.3.clone | custom fusion | bytes 49152 | tf_op jit(solution)/shard_map/jit(_take)/gather | solution.py:127
  304.0 23.0 %gather_fusion.5 = f32[4096]{0:T(1024)S(1)} fusion(f32[2048]{0:T(1024)S(1)} %bitcast.285, s32[4096]{0:T(1024)S(1)} %broadcast_clamp_fusion.11), kind=kCustom, calls=%fused_computation.4.clone | custom fusion | bytes 49152 | tf_op jit(solution)/shard_map/jit(_take)/gather | solution.py:127
  327.1 23.0 %gather_fusion.6 = f32[4096]{0:T(1024)S(1)} fusion(f32[2048]{0:T(1024)S(1)} %bitcast.286, s32[4096]{0:T(1024)S(1)} %broadcast_clamp_fusion.10), kind=kCustom, calls=%fused_computation.5.clone | custom fusion | bytes 49152 | tf_op jit(solution)/shard_map/jit(_take)/gather | solution.py:127
  350.2 23.0 %gather_fusion.7 = f32[4096]{0:T(1024)S(1)} fusion(f32[2048]{0:T(1024)S(1)} %bitcast.287, s32[4096]{0:T(1024)S(1)} %broadcast_clamp_fusion.9), kind=kCustom, calls=%fused_computation.6.clone | custom fusion | bytes 49152 | tf_op jit(solution)/shard_map/jit(_take)/gather | solution.py:127
  373.3 23.0 %gather_fusion.8 = f32[4096]{0:T(1024)S(1)} fusion(f32[2048]{0:T(1024)S(1)} %bitcast.288, s32[4096]{0:T(1024)S(1)} %broadcast_clamp_fusion.8), kind=kCustom, calls=%fused_computation.7.clone | custom fusion | bytes 49152 | tf_op jit(solution)/shard_map/jit(_take)/gather | solution.py:127
  396.4 23.0 %gather_fusion.9 = f32[4096]{0:T(1024)S(1)} fusion(f32[2048]{0:T(1024)S(1)} %bitcast.289, s32[4096]{0:T(1024)S(1)} %broadcast_clamp_fusion.7), kind=kCustom, calls=%fused_computation.8.clone | custom fusion | bytes 49152 | tf_op jit(solution)/shard_map/jit(_take)/gather | solution.py:128
  419.5 23.0 %gather_fusion.10 = f32[4096]{0:T(1024)S(1)} fusion(f32[2048]{0:T(1024)S(1)} %bitcast.290, s32[4096]{0:T(1024)S(1)} %broadcast_clamp_fusion.6), kind=kCustom, calls=%fused_computation.9.clone | custom fusion | bytes 49152 | tf_op jit(solution)/shard_map/jit(_take)/gather | solution.py:128
  442.5 23.0 %gather_fusion.11 = f32[4096]{0:T(1024)S(1)} fusion(f32[2048]{0:T(1024)S(1)} %bitcast.291, s32[4096]{0:T(1024)S(1)} %broadcast_clamp_fusion.5), kind=kCustom, calls=%fused_computation.10.clone | custom fusion | bytes 49152 | tf_op jit(solution)/shard_map/jit(_take)/gather | solution.py:128
  465.6 23.0 %gather_fusion.12 = f32[4096]{0:T(1024)S(1)} fusion(f32[2048]{0:T(1024)S(1)} %bitcast.292, s32[4096]{0:T(1024)S(1)} %broadcast_clamp_fusion.4), kind=kCustom, calls=%fused_computation.11.clone | custom fusion | bytes 49152 | tf_op jit(solution)/shard_map/jit(_take)/gather | solution.py:128
  488.7 23.0 %gather_fusion.13 = f32[4096]{0:T(1024)S(1)} fusion(f32[2048]{0:T(1024)S(1)} %bitcast.293, s32[4096]{0:T(1024)S(1)} %broadcast_clamp_fusion.3), kind=kCustom, calls=%fused_computation.12.clone | custom fusion | bytes 49152 | tf_op jit(solution)/shard_map/jit(_take)/gather | solution.py:128
  511.8 23.0 %gather_fusion.14 = f32[4096]{0:T(1024)S(1)} fusion(f32[2048]{0:T(1024)S(1)} %bitcast.294, s32[4096]{0:T(1024)S(1)} %broadcast_clamp_fusion.2), kind=kCustom, calls=%fused_computation.13.clone | custom fusion | bytes 49152 | tf_op jit(solution)/shard_map/jit(_take)/gather | solution.py:128
  534.9 23.0 %gather_fusion.15 = f32[4096]{0:T(1024)S(1)} fusion(f32[2048]{0:T(1024)S(1)} %bitcast.295, s32[4096]{0:T(1024)S(1)} %broadcast_clamp_fusion.1), kind=kCustom, calls=%fused_computation.14.clone | custom fusion | bytes 49152 | tf_op jit(solution)/shard_map/jit(_take)/gather | solution.py:128
  558.0 23.0 %gather_fusion.16 = f32[4096]{0:T(1024)S(1)} fusion(f32[2048]{0:T(1024)S(1)} %bitcast.296, s32[4096]{0:T(1024)S(1)} %broadcast_clamp_fusion), kind=kCustom, calls=%fused_computation.15.clone | custom fusion | bytes 49152 | tf_op jit(solution)/shard_map/jit(_take)/gather | solution.py:128
  581.3 10.0 %all_to_all.15 = f32[2,16,256]{2,0,1:T(2,128)S(1)} all-to-all(f32[2,16,256]{2,0,1:T(2,128)S(1)} %copy.25), channel_id=1, replica_groups=mesh['groups'=1,'col'=16,'facet'=1,'pol'=2] {'col'}, dimensions={1} | all-to-all | bytes 65536 | tf_op jit(solution)/shard_map/all_to_all | solution.py:132
  (226 shorter events, 169.4 us)
Async XLA Ops:
  16.8 19.5 %copy-start.2 = (s32[16]{0:T(128)S(1)}, s32[16]{0:T(128)}, u32[]{:S(2)}) copy-start(s32[16]{0:T(128)} %param.14) | copy-start | bytes 196
  16.8 21.9 %copy-start.1 = (f32[1,1,8,4096]{3,2,1,0:T(8,128)S(1)}, f32[1,1,8,4096]{3,2,1,0:T(8,128)}, u32[]{:S(2)}) copy-start(f32[1,1,8,4096]{3,2,1,0:T(8,128)} %param.12) | copy-start | bytes 393220
  18.1 182.7 %all-to-all-start.1 = ((f32[3,16,256]{2,0,1:T(4,128)}), f32[3,16,256]{2,0,1:T(4,128)S(1)}, u32[]{:S(2)}, u32[]{:S(2)}) async-start(f32[3,16,256]{2,0,1:T(4,128)} %copy.20), calls=%async_computation.1 | async-start | bytes 131072 | tf_op jit(solution)/shard_map/all_to_all | solution.py:112
  38.7 1.6 copy-start
  43.5 7.3 %collective-permute-start = (f32[8,256]{1,0:T(8,128)S(1)}, f32[8,256]{1,0:T(8,128)S(1)}, u32[]{:S(2)}, u32[]{:S(2)}) collective-permute-start(f32[8,256]{1,0:T(8,128)S(1)} %maximum_add_fusion.3), channel_id=1, source_target_pairs={{0,2},{2,4},{4,6},{6,8},{8,10},{10,12},{12,14},{14,16},{16,18},{18... | collective-permute-start | bytes 24584 | tf_op jit(solution)/shard_map/while/body/eval_jaxpr/ppermute | solution.py:18
  53.5 7.3 %collective-permute-start = (f32[8,256]{1,0:T(8,128)S(1)}, f32[8,256]{1,0:T(8,128)S(1)}, u32[]{:S(2)}, u32[]{:S(2)}) collective-permute-start(f32[8,256]{1,0:T(8,128)S(1)} %maximum_add_fusion.3), channel_id=1, source_target_pairs={{0,2},{2,4},{4,6},{6,8},{8,10},{10,12},{12,14},{14,16},{16,18},{18... | collective-permute-start | bytes 24584 | tf_op jit(solution)/shard_map/while/body/eval_jaxpr/ppermute | solution.py:18
  63.5 7.3 %collective-permute-start = (f32[8,256]{1,0:T(8,128)S(1)}, f32[8,256]{1,0:T(8,128)S(1)}, u32[]{:S(2)}, u32[]{:S(2)}) collective-permute-start(f32[8,256]{1,0:T(8,128)S(1)} %maximum_add_fusion.3), channel_id=1, source_target_pairs={{0,2},{2,4},{4,6},{6,8},{8,10},{10,12},{12,14},{14,16},{16,18},{18... | collective-permute-start | bytes 24584 | tf_op jit(solution)/shard_map/while/body/eval_jaxpr/ppermute | solution.py:18
  73.6 7.3 %collective-permute-start = (f32[8,256]{1,0:T(8,128)S(1)}, f32[8,256]{1,0:T(8,128)S(1)}, u32[]{:S(2)}, u32[]{:S(2)}) collective-permute-start(f32[8,256]{1,0:T(8,128)S(1)} %maximum_add_fusion.3), channel_id=1, source_target_pairs={{0,2},{2,4},{4,6},{6,8},{8,10},{10,12},{12,14},{14,16},{16,18},{18... | collective-permute-start | bytes 24584 | tf_op jit(solution)/shard_map/while/body/eval_jaxpr/ppermute | solution.py:18
  83.6 7.3 %collective-permute-start = (f32[8,256]{1,0:T(8,128)S(1)}, f32[8,256]{1,0:T(8,128)S(1)}, u32[]{:S(2)}, u32[]{:S(2)}) collective-permute-start(f32[8,256]{1,0:T(8,128)S(1)} %maximum_add_fusion.3), channel_id=1, source_target_pairs={{0,2},{2,4},{4,6},{6,8},{8,10},{10,12},{12,14},{14,16},{16,18},{18... | collective-permute-start | bytes 24584 | tf_op jit(solution)/shard_map/while/body/eval_jaxpr/ppermute | solution.py:18
  93.7 7.3 %collective-permute-start = (f32[8,256]{1,0:T(8,128)S(1)}, f32[8,256]{1,0:T(8,128)S(1)}, u32[]{:S(2)}, u32[]{:S(2)}) collective-permute-start(f32[8,256]{1,0:T(8,128)S(1)} %maximum_add_fusion.3), channel_id=1, source_target_pairs={{0,2},{2,4},{4,6},{6,8},{8,10},{10,12},{12,14},{14,16},{16,18},{18... | collective-permute-start | bytes 24584 | tf_op jit(solution)/shard_map/while/body/eval_jaxpr/ppermute | solution.py:18
  103.7 7.3 %collective-permute-start = (f32[8,256]{1,0:T(8,128)S(1)}, f32[8,256]{1,0:T(8,128)S(1)}, u32[]{:S(2)}, u32[]{:S(2)}) collective-permute-start(f32[8,256]{1,0:T(8,128)S(1)} %maximum_add_fusion.3), channel_id=1, source_target_pairs={{0,2},{2,4},{4,6},{6,8},{8,10},{10,12},{12,14},{14,16},{16,18},{18... | collective-permute-start | bytes 24584 | tf_op jit(solution)/shard_map/while/body/eval_jaxpr/ppermute | solution.py:18
  113.8 7.3 %collective-permute-start = (f32[8,256]{1,0:T(8,128)S(1)}, f32[8,256]{1,0:T(8,128)S(1)}, u32[]{:S(2)}, u32[]{:S(2)}) collective-permute-start(f32[8,256]{1,0:T(8,128)S(1)} %maximum_add_fusion.3), channel_id=1, source_target_pairs={{0,2},{2,4},{4,6},{6,8},{8,10},{10,12},{12,14},{14,16},{16,18},{18... | collective-permute-start | bytes 24584 | tf_op jit(solution)/shard_map/while/body/eval_jaxpr/ppermute | solution.py:18
  123.8 7.3 %collective-permute-start = (f32[8,256]{1,0:T(8,128)S(1)}, f32[8,256]{1,0:T(8,128)S(1)}, u32[]{:S(2)}, u32[]{:S(2)}) collective-permute-start(f32[8,256]{1,0:T(8,128)S(1)} %maximum_add_fusion.3), channel_id=1, source_target_pairs={{0,2},{2,4},{4,6},{6,8},{8,10},{10,12},{12,14},{14,16},{16,18},{18... | collective-permute-start | bytes 24584 | tf_op jit(solution)/shard_map/while/body/eval_jaxpr/ppermute | solution.py:18
  133.8 7.3 %collective-permute-start = (f32[8,256]{1,0:T(8,128)S(1)}, f32[8,256]{1,0:T(8,128)S(1)}, u32[]{:S(2)}, u32[]{:S(2)}) collective-permute-start(f32[8,256]{1,0:T(8,128)S(1)} %maximum_add_fusion.3), channel_id=1, source_target_pairs={{0,2},{2,4},{4,6},{6,8},{8,10},{10,12},{12,14},{14,16},{16,18},{18... | collective-permute-start | bytes 24584 | tf_op jit(solution)/shard_map/while/body/eval_jaxpr/ppermute | solution.py:18
  143.9 7.3 %collective-permute-start = (f32[8,256]{1,0:T(8,128)S(1)}, f32[8,256]{1,0:T(8,128)S(1)}, u32[]{:S(2)}, u32[]{:S(2)}) collective-permute-start(f32[8,256]{1,0:T(8,128)S(1)} %maximum_add_fusion.3), channel_id=1, source_target_pairs={{0,2},{2,4},{4,6},{6,8},{8,10},{10,12},{12,14},{14,16},{16,18},{18... | collective-permute-start | bytes 24584 | tf_op jit(solution)/shard_map/while/body/eval_jaxpr/ppermute | solution.py:18
  153.9 7.3 %collective-permute-start = (f32[8,256]{1,0:T(8,128)S(1)}, f32[8,256]{1,0:T(8,128)S(1)}, u32[]{:S(2)}, u32[]{:S(2)}) collective-permute-start(f32[8,256]{1,0:T(8,128)S(1)} %maximum_add_fusion.3), channel_id=1, source_target_pairs={{0,2},{2,4},{4,6},{6,8},{8,10},{10,12},{12,14},{14,16},{16,18},{18... | collective-permute-start | bytes 24584 | tf_op jit(solution)/shard_map/while/body/eval_jaxpr/ppermute | solution.py:18
  164.0 7.3 %collective-permute-start = (f32[8,256]{1,0:T(8,128)S(1)}, f32[8,256]{1,0:T(8,128)S(1)}, u32[]{:S(2)}, u32[]{:S(2)}) collective-permute-start(f32[8,256]{1,0:T(8,128)S(1)} %maximum_add_fusion.3), channel_id=1, source_target_pairs={{0,2},{2,4},{4,6},{6,8},{8,10},{10,12},{12,14},{14,16},{16,18},{18... | collective-permute-start | bytes 24584 | tf_op jit(solution)/shard_map/while/body/eval_jaxpr/ppermute | solution.py:18
  174.0 7.3 %collective-permute-start = (f32[8,256]{1,0:T(8,128)S(1)}, f32[8,256]{1,0:T(8,128)S(1)}, u32[]{:S(2)}, u32[]{:S(2)}) collective-permute-start(f32[8,256]{1,0:T(8,128)S(1)} %maximum_add_fusion.3), channel_id=1, source_target_pairs={{0,2},{2,4},{4,6},{6,8},{8,10},{10,12},{12,14},{14,16},{16,18},{18... | collective-permute-start | bytes 24584 | tf_op jit(solution)/shard_map/while/body/eval_jaxpr/ppermute | solution.py:18
  184.0 7.3 %collective-permute-start = (f32[8,256]{1,0:T(8,128)S(1)}, f32[8,256]{1,0:T(8,128)S(1)}, u32[]{:S(2)}, u32[]{:S(2)}) collective-permute-start(f32[8,256]{1,0:T(8,128)S(1)} %maximum_add_fusion.3), channel_id=1, source_target_pairs={{0,2},{2,4},{4,6},{6,8},{8,10},{10,12},{12,14},{14,16},{16,18},{18... | collective-permute-start | bytes 24584 | tf_op jit(solution)/shard_map/while/body/eval_jaxpr/ppermute | solution.py:18
  200.7 10.8 %all-to-all-start = ((s32[1,16,256]{2,0,1:T(1,128)}), s32[1,16,256]{2,0,1:T(1,128)S(1)}, u32[]{:S(2)}, u32[]{:S(2)}) async-start(s32[1,16,256]{2,0,1:T(1,128)} %bitcast.10), calls=%async_computation | async-start | bytes 32768 | tf_op jit(solution)/shard_map/all_to_all | solution.py:113
where the time goes:
time: 600 us; the launch traced here: 599 us
  local copies, waits for them, and re-layouts  403 us (67%)
  waiting for transfers between devices  114 us (19%)
  other arithmetic  48.5 us (8%)
  starting transfers between devices  14.8 us (2%)
  blocking collectives  9.98 us (2%)
  matrix products  6.14 us (1%)
    gather x16, local copies, waits for them, and re-layouts, body(): real_sum = real_sum + weight * jnp.take(flat_grid, row_start + clipped)  184 us
    gather x16, local copies, waits for them, and re-layouts, body(): imag_sum = imag_sum + weight * jnp.take(flat_grid, row_start + M + clipped)  184 us
    ppermute x15, waiting for transfers between devices, from_behind(): lax.ppermute(array, axis, [(i, (i + by) % peers) for i in range(peers)])  107 us
    neg x16, other arithmetic, column_term(): trig_rows = jnp.stack([jnp.cos(angles), -jnp.sin(angles)])  17.4 us
    another operation x4, other arithmetic  14.1 us
  transfers between devices with their start and end apart: 17, of which 16 were waited for; matrix products, arithmetic and copies ran while one was open for 11% of the time, Pallas kernels for 0%

commit v1 on v0

v1 whole, which is shorter than its diff:
```python
import functools
import math

import jax
import jax.numpy as jnp
import ml_dtypes
import numpy as np
from jax import lax
from jax.experimental import pallas as pl
from jax.experimental.pallas import tpu as pltpu
from jax.sharding import PartitionSpec as P

NIMG = 65536
M = 128
S = 8
TWO_PI = 2.0 * math.pi
MESH = pl.DeviceIdType.MESH


def dft_constant(pixels):
    places = np.arange(pixels, dtype=np.int64)[:, None]
    frequency = np.arange(M, dtype=np.int64)[None, :]
    angles = (places * frequency % NIMG).astype(np.float64) * (TWO_PI / NIMG)
    table = np.concatenate([np.cos(angles), -np.sin(angles)], axis=1)
    return table.astype(np.float32).astype(ml_dtypes.bfloat16)


def cos_sin(turns):
    quarter = (turns + NIMG // 8) >> 14
    x = (turns - (quarter << 14)).astype(jnp.float32) * (TWO_PI / NIMG)
    z = x * x
    sine = x + x * z * (-1.6666654611e-1 + z * (8.3321608736e-3 - z * 1.9515295891e-4))
    cosine = 1.0 - 0.5 * z + z * z * (
        4.166664568298827e-2 + z * (-1.388731625493765e-3 + z * 2.443315711809948e-5)
    )
    odd = (quarter & 1) == 1
    cos_sign = (1 - ((quarter + 1) & 2)).astype(jnp.float32)
    sin_sign = (1 - (quarter & 2)).astype(jnp.float32)
    return jnp.where(odd, sine, cosine) * cos_sign, jnp.where(odd, cosine, sine) * sin_sign


def kernel(
    n,
    facets,
    facet_offset,
    offsets,
    row_count,
    dest,
    grid_row,
    position,
    observed,
    table_hbm,
    grid_out,
    residual,
    table,
    cos_ref,
    sin_ref,
    modulated,
    turn_cos,
    turn_sin,
    terms,
    arrived,
    grid,
    one_hot,
    weights,
    table_sem,
    send1,
    recv1,
    send2,
    recv2,
):
    me = lax.axis_index("col")
    rows, pixels = facets.shape[2], facets.shape[3]
    peers = [lax.rem(me + d, n) for d in range(n)]

    load = pltpu.make_async_copy(table_hbm, table, table_sem)
    load.start()
    barrier = pltpu.get_barrier_semaphore()
    for d in range(1, n):
        pl.semaphore_signal(barrier, inc=1, device_id={"col": peers[d]}, device_id_type=MESH)

    spot = lax.broadcasted_iota(jnp.int32, (n, 128), 0)
    lane = lax.broadcasted_iota(jnp.int32, (n, 128), 1)
    offset = jnp.zeros((n, 128), jnp.int32)
    for d in range(n):
        offset = jnp.where(spot == d, offsets[peers[d]], offset)
    turn = (facet_offset[0] * ((offset + lane) & (NIMG - 1))) & (NIMG - 1)
    cosine, sine = cos_sin(turn)
    norm_factor = 1.0 / math.sqrt(NIMG)
    turn_cos[...] = cosine * norm_factor
    turn_sin[...] = -sine * norm_factor

    for j in range(pixels // 128):
        cosine, sine = cos_sin(((lane + j * 128) * offset) & (NIMG - 1))
        cos_ref[:, j * 128 : (j + 1) * 128] = cosine
        sin_ref[:, j * 128 : (j + 1) * 128] = -sine

    step = 1024
    for j in range(pixels // step):
        cut = slice(j * step, (j + 1) * step)
        places = (lax.broadcasted_iota(jnp.int32, (rows, step), 1) + j * step).astype(jnp.float32)
        x = (2.0 * places + 1.0) / pixels - 1.0
        squared = 1.0 - x * x
        scaled = facets[0, 0, :, cut] * (squared * squared)
        for d in range(n):
            modulated[2 * rows * d : 2 * rows * (d + 1), cut] = jnp.concatenate(
                [scaled * cos_ref[d : d + 1, cut], scaled * sin_ref[d : d + 1, cut]], axis=0
            ).astype(jnp.bfloat16)

    load.wait()
    product = jnp.dot(modulated[...], table[...], preferred_element_type=jnp.float32)
    for d in range(n):
        upper = product[2 * rows * d : 2 * rows * d + rows]
        lower = product[2 * rows * d + rows : 2 * rows * (d + 1)]
        real_part = upper[:, :M] - lower[:, M:]
        imag_part = upper[:, M:] + lower[:, :M]
        ct, st = turn_cos[d : d + 1, :], turn_sin[d : d + 1, :]
        terms[d, :, :M] = real_part * ct - imag_part * st
        terms[d, :, M:] = real_part * st + imag_part * ct

    pl.semaphore_wait(barrier, n - 1)

    def scatter_copy(d):
        return pltpu.make_async_remote_copy(
            src_ref=terms.at[d],
            dst_ref=arrived.at[d],
            send_sem=send1.at[d],
            recv_sem=recv1.at[d],
            device_id={"col": peers[d]},
            device_id_type=MESH,
        )

    for d in range(1, n):
        scatter_copy(d).start()

    total_rows = n * rows
    for j in range(dest.shape[0]):
        cut = slice(j * 128, (j + 1) * 128)
        wanted = dest[j : j + 1, :] * rows + grid_row[j : j + 1, :]
        hot = (lax.broadcasted_iota(jnp.int32, (total_rows, 128), 0) == wanted).astype(jnp.float32)
        hot = hot.astype(jnp.bfloat16)
        one_hot[:total_rows, cut] = hot
        one_hot[total_rows:, cut] = hot
        cell = lax.broadcasted_iota(jnp.int32, (M, 128), 0).astype(jnp.float32)
        r = (cell - position[j : j + 1, :]) * (2.0 / S)
        tap = jnp.maximum(1.0 - r * r, 0.0)
        weights[:, cut] = tap * tap

    total = terms[0]
    for d in range(1, n):
        scatter_copy(d).wait_recv()
        total = total + arrived[d]
    grid[pl.ds(me, 1)] = total[None]
    grid_out[0, 0] = total

    def gather_copy(d):
        return pltpu.make_async_remote_copy(
            src_ref=grid.at[me],
            dst_ref=grid.at[me],
            send_sem=send2.at[d],
            recv_sem=recv2.at[d],
            device_id={"col": peers[d]},
            device_id_type=MESH,
        )

    for d in range(1, n):
        gather_copy(d).start()
    for d in range(1, n):
        scatter_copy(d).wait_send()
    for d in range(1, n):
        gather_copy(d).wait_recv()

    turned = grid[...].reshape(total_rows, 2 * M).T
    high = turned.astype(jnp.bfloat16)
    low = (turned - high.astype(jnp.float32)).astype(jnp.bfloat16)
    left = jnp.concatenate([high, low], axis=1)
    live_count = row_count[0]
    step = 256
    for j in range(residual.shape[2] // step):
        cut = slice(j * step, (j + 1) * step)
        picked = jnp.dot(left, one_hot[:, cut], preferred_element_type=jnp.float32)
        w = weights[:, cut]
        real_sum = jnp.sum(picked[:M] * w, axis=0, keepdims=True)
        imag_sum = jnp.sum(picked[M:] * w, axis=0, keepdims=True)
        live = lax.broadcasted_iota(jnp.int32, (1, step), 1) + j * step < live_count
        residual[0, 0:1, cut] = jnp.where(live, observed[0, 0:1, cut] - real_sum, 0.0)
        residual[0, 1:2, cut] = jnp.where(live, observed[0, 1:2, cut] - imag_sum, 0.0)

    for d in range(1, n):
        gather_copy(d).wait_send()


def body(
    facets, facet_offsets, subgrid_offsets, row_counts, dest_column, grid_row, position, observed
):
    n = lax.axis_size("col")
    rows, pixels = facets.shape[2], facets.shape[3]
    count = dest_column.shape[0]
    tall = (count // 128, 128)
    vmem = pl.BlockSpec(memory_space=pltpu.VMEM)
    smem = pl.BlockSpec(memory_space=pltpu.SMEM)
    f32, bf16 = jnp.float32, jnp.bfloat16
    return pl.pallas_call(
        functools.partial(kernel, n),
        out_shape=(
            jax.ShapeDtypeStruct((1, 1, rows, 2 * M), f32),
            jax.ShapeDtypeStruct(observed.shape, f32),
        ),
        in_specs=[vmem, smem, smem, smem, vmem, vmem, vmem, vmem, pl.BlockSpec(memory_space=pl.ANY)],
        out_specs=(vmem, vmem),
        scratch_shapes=[
            pltpu.VMEM((pixels, 2 * M), bf16),
            pltpu.VMEM((n, pixels), f32),
            pltpu.VMEM((n, pixels), f32),
            pltpu.VMEM((2 * rows * n, pixels), bf16),
            pltpu.VMEM((n, M), f32),
            pltpu.VMEM((n, M), f32),
            pltpu.VMEM((n, rows, 2 * M), f32),
            pltpu.VMEM((n, rows, 2 * M), f32),
            pltpu.VMEM((n, rows, 2 * M), f32),
            pltpu.VMEM((2 * n * rows, count), bf16),
            pltpu.VMEM((M, count), f32),
            pltpu.SemaphoreType.DMA,
            pltpu.SemaphoreType.DMA((n,)),
            pltpu.SemaphoreType.DMA((n,)),
            pltpu.SemaphoreType.DMA((n,)),
            pltpu.SemaphoreType.DMA((n,)),
        ],
        compiler_params=pltpu.CompilerParams(
            collective_id=0, has_side_effects=True, vmem_limit_bytes=48 * 1024 * 1024
        ),
    )(
        facets,
        facet_offsets,
        subgrid_offsets,
        row_counts,
        dest_column.reshape(tall),
        grid_row.reshape(tall),
        position.reshape(tall),
        observed,
        jnp.asarray(dft_constant(pixels)),
    )


def solution(mesh):
    placed = (
        P(("groups", "col"), "pol", "facet", None),
        P(("groups", "col")),
        P("groups"),
        P(("groups", "col", "facet")),
        P(("groups", "col", "facet")),
        P(("groups", "col", "facet")),
        P(("groups", "col", "facet")),
        P("pol", None, ("groups", "col", "facet")),
    )
    return jax.shard_map(
        body,
        mesh=mesh,
        in_specs=placed,
        out_specs=(
            P(("groups", "col"), "pol", "facet", None),
            P("pol", None, ("groups", "col", "facet")),
        ),
        check_vma=False,
    )
```

time: 600 us -> 28.8 us (0.05)
  local copies, waits for them, and re-layouts: 403 us -> 7.16 us
  waiting for transfers between devices: 114 us -> 0 us
  other arithmetic: 48.5 us -> 0 us
  Pallas kernels: 0 us -> 19.3 us
  starting transfers between devices: 14.8 us -> 0 us
  blocking collectives: 9.98 us -> 0 us
  matrix products: 6.14 us -> 0 us
    gather x33 -> x0, local copies, waits for them, and re-layouts: 374 us -> none  [the longest x16 184 us: body(): real_sum = real_sum + weight * jnp.take(flat_grid, row_start + clipped)]
    ppermute x15 -> x0, waiting for transfers between devices: 107 us -> none  [from_behind(): lax.ppermute(array, axis, [(i, (i + by) % peers) for i in range(peers)])]
    pallas_call x0 -> x1, Pallas kernels: none -> 19.3 us  [body(): pl.pallas_call(functools.partial(kernel, n), out_shape=(jax.ShapeDtypeStr...]
    neg x16 -> x0, other arithmetic: 17.4 us -> none  [column_term(): trig_rows = jnp.stack([jnp.cos(angles), -jnp.sin(angles)])]
    another operation x24 -> x0, other arithmetic: 15.5 us -> none
    scatter x2 -> x0, local copies, waits for them, and re-layouts: 14.9 us -> none  [the longest x1 8.78 us: body(): targets = jnp.full((1, owners * capacity), -1, jnp.int32).at[:, slot_inde...]
    all_to_all x2 -> x0, starting transfers between devices: 12 us -> none  [the longest x1 8.31 us: body(): lax.all_to_all(outgoing, 'col', split_axis=1, concat_axis=1, tiled=True)]
    mul x18 -> x0, other arithmetic: 10 us -> none  [the longest x16 10 us: column_term(): sin_turn = -jnp.sin(rotation) * norm_factor]
  transfers between devices with their start and end apart: 17 -> 0, of which waited for: 16 -> 0; matrix products, arithmetic and copies ran while one was open for 11% -> 0% of each run, Pallas kernels for 0% -> 0%
where the time goes in v1:
time: 28.8 us; the launch traced here: 28.4 us
  Pallas kernels  19.3 us (67%)
  local copies, waits for them, and re-layouts  7.16 us (25%)
  between operations  1.95 us (7%)
    pallas_call x1, Pallas kernels, body(): pl.pallas_call(functools.partial(kernel, n), out_shape=(jax.ShapeDtypeStr...  19.3 us
    unnamed x16, local copies, waits for them, and re-layouts  7.16 us

profile of v1, /device:TPU:0, one launch (start us, length us, event | category | flops | bytes accessed | tf_op | source)
XLA Modules:
  0.0 28.4 jit_solution(5036541737495399889)
XLA Ops:
  1.9 0.0 copy-start
  1.9 1.6 %copy-done = bf16[4096,256]{1,0:T(8,128)(2,1)S(1)} copy-done((bf16[4096,256]{1,0:T(8,128)(2,1)S(1)}, bf16[4096,256]{1,0:T(8,128)(2,1)}, u32[]{:S(2)}) %copy-start) | copy-done | bytes 2097176
  3.5 0.0 copy-start.1
  3.5 0.9 %copy-done.1 = f32[1,1,8,4096]{3,2,1,0:T(8,128)S(1)} copy-done((f32[1,1,8,4096]{3,2,1,0:T(8,128)S(1)}, f32[1,1,8,4096]{3,2,1,0:T(8,128)}, u32[]{:S(2)}) %copy-start.1) | copy-done | bytes 131096
  4.4 0.0 copy-start.2
  4.4 0.7 %copy-done.2 = f32[1,2,2048]{2,1,0:T(2,128)S(1)} copy-done((f32[1,2,2048]{2,1,0:T(2,128)S(1)}, f32[1,2,2048]{2,1,0:T(2,128)}, u32[]{:S(2)}) %copy-start.2) | copy-done | bytes 16408
  5.1 0.0 copy-start.3
  5.1 0.7 %copy-done.3 = s32[2048]{0:T(1024)S(1)} copy-done((s32[2048]{0:T(1024)S(1)}, s32[2048]{0:T(1024)}, u32[]{:S(2)}) %copy-start.3) | copy-done | bytes 8216
  5.8 0.0 copy-start.4
  5.8 0.7 %copy-done.4 = s32[2048]{0:T(1024)S(1)} copy-done((s32[2048]{0:T(1024)S(1)}, s32[2048]{0:T(1024)}, u32[]{:S(2)}) %copy-start.4) | copy-done | bytes 8216
  6.5 0.0 copy-start.5
  6.5 0.7 %copy-done.5 = f32[2048]{0:T(1024)S(1)} copy-done((f32[2048]{0:T(1024)S(1)}, f32[2048]{0:T(1024)}, u32[]{:S(2)}) %copy-start.5) | copy-done | bytes 8216
  7.2 0.0 copy-start.6
  7.2 0.7 %copy-done.6 = s32[16]{0:T(128)S(1)} copy-done((s32[16]{0:T(128)S(1)}, s32[16]{0:T(128)}, u32[]{:S(2)}) %copy-start.6) | copy-done | bytes 88
  7.9 19.3 %shard_map.104 = (f32[1,1,8,256]{3,2,1,0:T(8,128)S(1)}, f32[1,2,2048]{2,1,0:T(2,128)S(1)}) custom-call(f32[1,1,8,4096]{3,2,1,0:T(8,128)S(1)} %copy-done.1, s32[1]{0:T(128)S(6)} %copy.13.facet_offset, s32[16]{0:T(128)S(1)} %copy-done.6, s32[1]{0:T(128)S(6)} %copy.14.row_count, s32[16,128]{1,0:T(8,128)S(1)} %bitcast.3, s32[16,128]{1,0:T(8,128)S(1)} %bitcast.4, ...), custom_call_target="tpu_custom_call" | custom-call | tf_op jit(solution)/shard_map/pallas_call | solution.py:203
  27.2 0.6 %copy.15 = f32[1,1,8,256]{3,2,1,0:T(8,128)} copy(f32[1,1,8,256]{3,2,1,0:T(8,128)S(1)} %get-tuple-element.4) | data formatting | bytes 16384
  27.8 0.6 %copy.16 = f32[1,2,2048]{2,1,0:T(2,128)} copy(f32[1,2,2048]{2,1,0:T(2,128)S(1)} %get-tuple-element.5) | data formatting | bytes 32768
Async XLA Ops:
  1.9 1.6 %copy-start = (bf16[4096,256]{1,0:T(8,128)(2,1)S(1)}, bf16[4096,256]{1,0:T(8,128)(2,1)}, u32[]{:S(2)}) copy-start(bf16[4096,256]{1,0:T(8,128)(2,1)} %constant.2.clone.table_hbm) | copy-start | bytes 6291460
  3.5 0.9 %copy-start.1 = (f32[1,1,8,4096]{3,2,1,0:T(8,128)S(1)}, f32[1,1,8,4096]{3,2,1,0:T(8,128)}, u32[]{:S(2)}) copy-start(f32[1,1,8,4096]{3,2,1,0:T(8,128)} %facets.1) | copy-start | bytes 393220
  4.4 0.7 %copy-start.2 = (f32[1,2,2048]{2,1,0:T(2,128)S(1)}, f32[1,2,2048]{2,1,0:T(2,128)}, u32[]{:S(2)}) copy-start(f32[1,2,2048]{2,1,0:T(2,128)} %observed.1) | copy-start | bytes 49156
  5.1 0.7 %copy-start.3 = (s32[2048]{0:T(1024)S(1)}, s32[2048]{0:T(1024)}, u32[]{:S(2)}) copy-start(s32[2048]{0:T(1024)} %param.13) | copy-start | bytes 24580
  5.8 0.7 %copy-start.4 = (s32[2048]{0:T(1024)S(1)}, s32[2048]{0:T(1024)}, u32[]{:S(2)}) copy-start(s32[2048]{0:T(1024)} %param.14) | copy-start | bytes 24580
  6.5 0.7 %copy-start.5 = (f32[2048]{0:T(1024)S(1)}, f32[2048]{0:T(1024)}, u32[]{:S(2)}) copy-start(f32[2048]{0:T(1024)} %param.15) | copy-start | bytes 24580
  7.2 0.7 %copy-start.6 = (s32[16]{0:T(128)S(1)}, s32[16]{0:T(128)}, u32[]{:S(2)}) copy-start(s32[16]{0:T(128)} %offsets.1) | copy-start | bytes 196

commit v2 on v1

v2 whole, which is shorter than its diff:
```python
import functools
import math

import jax
import jax.numpy as jnp
import ml_dtypes
import numpy as np
from jax import lax
from jax.experimental import pallas as pl
from jax.experimental.pallas import tpu as pltpu
from jax.sharding import PartitionSpec as P

NIMG = 65536
M = 128
S = 8
NEAR = 4
TWO_PI = 2.0 * math.pi
MESH = pl.DeviceIdType.MESH


def dft_constant(pixels):
    places = np.arange(pixels, dtype=np.int64)[:, None]
    frequency = np.arange(M, dtype=np.int64)[None, :]
    angles = (places * frequency % NIMG).astype(np.float64) * (TWO_PI / NIMG)
    table = np.concatenate([np.cos(angles), -np.sin(angles)], axis=1)
    return table.astype(np.float32).astype(ml_dtypes.bfloat16)


def cos_sin(turns):
    quarter = (turns + NIMG // 8) >> 14
    x = (turns - (quarter << 14)).astype(jnp.float32) * (TWO_PI / NIMG)
    z = x * x
    sine = x + x * z * (-1.6666654611e-1 + z * (8.3321608736e-3 - z * 1.9515295891e-4))
    cosine = 1.0 - 0.5 * z + z * z * (
        4.166664568298827e-2 + z * (-1.388731625493765e-3 + z * 2.443315711809948e-5)
    )
    odd = (quarter & 1) == 1
    cos_sign = (1 - ((quarter + 1) & 2)).astype(jnp.float32)
    sin_sign = (1 - (quarter & 2)).astype(jnp.float32)
    return jnp.where(odd, sine, cosine) * cos_sign, jnp.where(odd, cosine, sine) * sin_sign


def kernel(
    n,
    *refs,
):
    sources, (grid_out, residual_out), local, rest = refs[:9], refs[9:11], refs[11:20], refs[20:]
    facet_offset, offsets, row_count, facets, dest, grid_row, position, observed, table = local
    cos_ref, sin_ref, modulated, turn_cos, turn_sin, terms, arrived, grid, one_hot, weights = rest[:10]
    arrived_far, partial, residual = rest[10:13]
    load_sem, store_sem, send1, recv1, send2, recv2, send3, recv3 = rest[13:]
    me = lax.axis_index("col")
    rows, pixels = facets.shape[2], facets.shape[3]
    near = NEAR
    far = n // near
    high, low = me // near, lax.rem(me, near)
    near_peers = [high * near + lax.rem(low + d, near) for d in range(near)]
    far_peers = [lax.rem(high + e, far) * near + low for e in range(far)]
    columns = [near * h + lax.rem(low + d, near) for d in range(near) for h in range(far)]

    loads = [
        pltpu.make_async_copy(source, target, load_sem.at[i])
        for i, (source, target) in enumerate(zip(sources, local))
    ]
    for load in loads:
        load.start()
    barrier = pltpu.get_barrier_semaphore()
    for peer in near_peers[1:] + far_peers[1:]:
        pl.semaphore_signal(barrier, inc=1, device_id={"col": peer}, device_id_type=MESH)

    loads[0].wait()
    loads[1].wait()
    spot = lax.broadcasted_iota(jnp.int32, (n, 128), 0)
    lane = lax.broadcasted_iota(jnp.int32, (n, 128), 1)
    offset = jnp.zeros((n, 128), jnp.int32)
    for d in range(n):
        offset = jnp.where(spot == d, offsets[columns[d]], offset)
    turn = (facet_offset[0] * ((offset + lane) & (NIMG - 1))) & (NIMG - 1)
    cosine, sine = cos_sin(turn)
    norm_factor = 1.0 / math.sqrt(NIMG)
    turn_cos[...] = cosine * norm_factor
    turn_sin[...] = -sine * norm_factor

    for j in range(pixels // 128):
        cosine, sine = cos_sin(((lane + j * 128) * offset) & (NIMG - 1))
        cos_ref[:, j * 128 : (j + 1) * 128] = cosine
        sin_ref[:, j * 128 : (j + 1) * 128] = -sine

    loads[3].wait()
    step = 1024
    for j in range(pixels // step):
        cut = slice(j * step, (j + 1) * step)
        places = (lax.broadcasted_iota(jnp.int32, (rows, step), 1) + j * step).astype(jnp.float32)
        x = (2.0 * places + 1.0) / pixels - 1.0
        squared = 1.0 - x * x
        scaled = facets[0, 0, :, cut] * (squared * squared)
        for d in range(n):
            modulated[2 * rows * d : 2 * rows * (d + 1), cut] = jnp.concatenate(
                [scaled * cos_ref[d : d + 1, cut], scaled * sin_ref[d : d + 1, cut]], axis=0
            ).astype(jnp.bfloat16)

    loads[8].wait()
    product = jnp.dot(modulated[...], table[...], preferred_element_type=jnp.float32)
    for d in range(n):
        upper = product[2 * rows * d : 2 * rows * d + rows]
        lower = product[2 * rows * d + rows : 2 * rows * (d + 1)]
        real_part = upper[:, :M] - lower[:, M:]
        imag_part = upper[:, M:] + lower[:, :M]
        ct, st = turn_cos[d : d + 1, :], turn_sin[d : d + 1, :]
        terms[d // far, d % far, :, :M] = real_part * ct - imag_part * st
        terms[d // far, d % far, :, M:] = real_part * st + imag_part * ct

    pl.semaphore_wait(barrier, near + far - 2)

    def send(source, target, send_sem, recv_sem, peer):
        return pltpu.make_async_remote_copy(
            src_ref=source,
            dst_ref=target,
            send_sem=send_sem,
            recv_sem=recv_sem,
            device_id={"col": peer},
            device_id_type=MESH,
        )

    def first_copy(d, h):
        return send(terms.at[d, h], arrived.at[d, h], send1.at[d, h], recv1.at[d, h], near_peers[d])

    def second_copy(e, h):
        return send(
            partial.at[h], arrived_far.at[e, h], send2.at[e, h], recv2.at[e, h], far_peers[e]
        )

    def third_copy(d, h):
        here = grid.at[near * h + low]
        return send(here, here, send3.at[d, h], recv3.at[d, h], near_peers[d])

    for h in range(far):
        for d in range(1, near):
            first_copy(d, h).start()

    for load in loads[4:8]:
        load.wait()
    loads[2].wait()
    total_rows = n * rows
    for j in range(dest.shape[0]):
        cut = slice(j * 128, (j + 1) * 128)
        wanted = dest[j : j + 1, :] * rows + grid_row[j : j + 1, :]
        hot = (lax.broadcasted_iota(jnp.int32, (total_rows, 128), 0) == wanted).astype(jnp.float32)
        hot = hot.astype(jnp.bfloat16)
        one_hot[:total_rows, cut] = hot
        one_hot[total_rows:, cut] = hot
        cell = lax.broadcasted_iota(jnp.int32, (M, 128), 0).astype(jnp.float32)
        r = (cell - position[j : j + 1, :]) * (2.0 / S)
        tap = jnp.maximum(1.0 - r * r, 0.0)
        weights[:, cut] = tap * tap

    for h in range(far):
        total = terms[0, h]
        for d in range(1, near):
            first_copy(d, h).wait_recv()
            total = total + arrived[d, h]
        partial[h] = total
        for e in range(1, far):
            second_copy(e, h).start()
    for h in range(far):
        total = partial[h]
        for e in range(1, far):
            second_copy(e, h).wait_recv()
            total = total + arrived_far[e, h]
        grid[pl.ds(near * h + low, 1)] = total[None]
        for d in range(1, near):
            third_copy(d, h).start()
    stores = [pltpu.make_async_copy(grid.at[me], grid_out.at[0, 0], store_sem.at[0])]
    stores[0].start()
    for h in range(far):
        for d in range(1, near):
            first_copy(d, h).wait_send()
        for e in range(1, far):
            second_copy(e, h).wait_send()
    for h in range(far):
        for d in range(1, near):
            third_copy(d, h).wait_recv()

    turned = grid[...].reshape(total_rows, 2 * M).T
    coarse = turned.astype(jnp.bfloat16)
    fine = (turned - coarse.astype(jnp.float32)).astype(jnp.bfloat16)
    left = jnp.concatenate([coarse, fine], axis=1)
    live_count = row_count[0]
    step = 256
    for j in range(residual.shape[2] // step):
        cut = slice(j * step, (j + 1) * step)
        picked = jnp.dot(left, one_hot[:, cut], preferred_element_type=jnp.float32)
        w = weights[:, cut]
        real_sum = jnp.sum(picked[:M] * w, axis=0, keepdims=True)
        imag_sum = jnp.sum(picked[M:] * w, axis=0, keepdims=True)
        live = lax.broadcasted_iota(jnp.int32, (1, step), 1) + j * step < live_count
        residual[0, 0:1, cut] = jnp.where(live, observed[0, 0:1, cut] - real_sum, 0.0)
        residual[0, 1:2, cut] = jnp.where(live, observed[0, 1:2, cut] - imag_sum, 0.0)

    stores.append(pltpu.make_async_copy(residual, residual_out, store_sem.at[1]))
    stores[1].start()
    for h in range(far):
        for d in range(1, near):
            third_copy(d, h).wait_send()
    for store in stores:
        store.wait()


def body(
    facets, facet_offsets, subgrid_offsets, row_counts, dest_column, grid_row, position, observed
):
    n = lax.axis_size("col")
    far = n // NEAR
    rows, pixels = facets.shape[2], facets.shape[3]
    count = dest_column.shape[0]
    tall = (count // 128, 128)
    hbm = pl.BlockSpec(memory_space=pltpu.HBM)
    f32, bf16 = jnp.float32, jnp.bfloat16
    arrays = (
        facet_offsets,
        subgrid_offsets,
        row_counts,
        facets,
        dest_column.reshape(tall),
        grid_row.reshape(tall),
        position.reshape(tall),
        observed,
        jnp.asarray(dft_constant(pixels)),
    )
    spaces = [pltpu.SMEM] * 3 + [pltpu.VMEM] * 6
    shapes = (
        jax.ShapeDtypeStruct((1, 1, rows, 2 * M), f32),
        jax.ShapeDtypeStruct(observed.shape, f32),
    )
    return pl.pallas_call(
        functools.partial(kernel, n),
        out_shape=shapes,
        in_specs=[hbm] * len(arrays),
        out_specs=(hbm, hbm),
        scratch_shapes=[
            *[space(array.shape, array.dtype) for space, array in zip(spaces, arrays)],
            pltpu.VMEM((n, pixels), f32),
            pltpu.VMEM((n, pixels), f32),
            pltpu.VMEM((2 * rows * n, pixels), bf16),
            pltpu.VMEM((n, M), f32),
            pltpu.VMEM((n, M), f32),
            pltpu.VMEM((NEAR, far, rows, 2 * M), f32),
            pltpu.VMEM((NEAR, far, rows, 2 * M), f32),
            pltpu.VMEM((n, rows, 2 * M), f32),
            pltpu.VMEM((2 * n * rows, count), bf16),
            pltpu.VMEM((M, count), f32),
            pltpu.VMEM((far, far, rows, 2 * M), f32),
            pltpu.VMEM((far, rows, 2 * M), f32),
            pltpu.VMEM(observed.shape, f32),
            pltpu.SemaphoreType.DMA((len(arrays),)),
            pltpu.SemaphoreType.DMA((2,)),
            pltpu.SemaphoreType.DMA((NEAR, far)),
            pltpu.SemaphoreType.DMA((NEAR, far)),
            pltpu.SemaphoreType.DMA((far, far)),
            pltpu.SemaphoreType.DMA((far, far)),
            pltpu.SemaphoreType.DMA((NEAR, far)),
            pltpu.SemaphoreType.DMA((NEAR, far)),
        ],
        compiler_params=pltpu.CompilerParams(
            collective_id=0, has_side_effects=True, vmem_limit_bytes=64 * 1024 * 1024
        ),
    )(*arrays)


def solution(mesh):
    placed = (
        P(("groups", "col"), "pol", "facet", None),
        P(("groups", "col")),
        P("groups"),
        P(("groups", "col", "facet")),
        P(("groups", "col", "facet")),
        P(("groups", "col", "facet")),
        P(("groups", "col", "facet")),
        P("pol", None, ("groups", "col", "facet")),
    )
    return jax.shard_map(
        body,
        mesh=mesh,
        in_specs=placed,
        out_specs=(
            P(("groups", "col"), "pol", "facet", None),
            P("pol", None, ("groups", "col", "facet")),
        ),
        check_vma=False,
    )
```

time: 28.8 us -> 23.8 us (0.83)
  local copies, waits for them, and re-layouts: 7.16 us -> 2.62 us
  Pallas kernels: 19.3 us -> 18.9 us
    unnamed x16 -> x2, local copies, waits for them, and re-layouts: 7.16 us -> 2.62 us
    pallas_call x1, Pallas kernels: 19.3 us -> 18.9 us  [body(): pl.pallas_call(functools.partial(kernel, n), out_shape=shapes, in_specs=[...]
where the time goes in v2:
time: 23.8 us; the launch traced here: 23.5 us
  Pallas kernels  18.9 us (79%)
  local copies, waits for them, and re-layouts  2.62 us (11%)
  between operations  1.93 us (8%)
    pallas_call x1, Pallas kernels, body(): pl.pallas_call(functools.partial(kernel, n), out_shape=shapes, in_specs=[...  18.9 us
    unnamed x2, local copies, waits for them, and re-layouts  2.62 us

profile of v2, /device:TPU:0, one launch (start us, length us, event | category | flops | bytes accessed | tf_op | source)
XLA Modules:
  0.0 23.5 jit_solution(10241566254661650645)
XLA Ops:
  1.9 18.9 %shard_map.104 = (f32[1,1,8,256]{3,2,1,0:T(8,128)}, f32[1,2,2048]{2,1,0:T(2,128)}) custom-call(s32[1]{0:T(128)S(6)} %copy.13.refs_0_, s32[16]{0:T(128)} %refs_1_.1, s32[1]{0:T(128)S(6)} %copy.14.refs_2_, f32[1,1,8,4096]{3,2,1,0:T(8,128)} %refs_3_.1, s32[16,128]{1,0:T(8,128)} %bitcast.3, s32[16,128]{1,0:T(8,128)} %bitcast.4, f32[16,128]{1,0:T(8,128)} %bitcast.5, ...), custom_call_target="tpu_custom_call" | custom-call | tf_op jit(solution)/shard_map/pallas_call | solution.py:235
  20.9 1.3 %copy.15 = f32[1,1,8,256]{3,2,1,0:T(8,128)} copy(f32[1,1,8,256]{3,2,1,0:T(8,128)} %get-tuple-element.4) | data formatting | bytes 16384
  22.2 1.3 %copy.16 = f32[1,2,2048]{2,1,0:T(2,128)} copy(f32[1,2,2048]{2,1,0:T(2,128)} %get-tuple-element.5) | data formatting | bytes 32768

commit v3 on v2

--- a/solution.py
+++ b/solution.py
@@ -44,11 +44,12 @@
     n,
     *refs,
 ):
-    sources, (grid_out, residual_out), local, rest = refs[:9], refs[9:11], refs[11:20], refs[20:]
-    facet_offset, offsets, row_count, facets, dest, grid_row, position, observed, table = local
+    sources, (grid_out, residual), local, rest = refs[:9], refs[9:11], refs[11:18], refs[18:]
+    facet_offset, row_count = sources[:2]
+    offsets, facets, dest, grid_row, position, observed, table = local
     cos_ref, sin_ref, modulated, turn_cos, turn_sin, terms, arrived, grid, one_hot, weights = rest[:10]
-    arrived_far, partial, residual = rest[10:13]
-    load_sem, store_sem, send1, recv1, send2, recv2, send3, recv3 = rest[13:]
+    arrived_far, partial = rest[10:12]
+    load_sem, send1, recv1, send2, recv2, send3, recv3 = rest[12:]
     me = lax.axis_index("col")
     rows, pixels = facets.shape[2], facets.shape[3]
     near = NEAR
@@ -60,7 +61,7 @@
 
     loads = [
         pltpu.make_async_copy(source, target, load_sem.at[i])
-        for i, (source, target) in enumerate(zip(sources, local))
+        for i, (source, target) in enumerate(zip(sources[2:], local))
     ]
     for load in loads:
         load.start()
@@ -69,7 +70,6 @@
         pl.semaphore_signal(barrier, inc=1, device_id={"col": peer}, device_id_type=MESH)
 
     loads[0].wait()
-    loads[1].wait()
     spot = lax.broadcasted_iota(jnp.int32, (n, 128), 0)
     lane = lax.broadcasted_iota(jnp.int32, (n, 128), 1)
     offset = jnp.zeros((n, 128), jnp.int32)
@@ -86,7 +86,7 @@
         cos_ref[:, j * 128 : (j + 1) * 128] = cosine
         sin_ref[:, j * 128 : (j + 1) * 128] = -sine
 
-    loads[3].wait()
+    loads[1].wait()
     step = 1024
     for j in range(pixels // step):
         cut = slice(j * step, (j + 1) * step)
@@ -99,7 +99,7 @@
                 [scaled * cos_ref[d : d + 1, cut], scaled * sin_ref[d : d + 1, cut]], axis=0
             ).astype(jnp.bfloat16)
 
-    loads[8].wait()
+    loads[6].wait()
     product = jnp.dot(modulated[...], table[...], preferred_element_type=jnp.float32)
     for d in range(n):
         upper = product[2 * rows * d : 2 * rows * d + rows]
@@ -122,29 +122,26 @@
             device_id_type=MESH,
         )
 
-    def first_copy(d, h):
-        return send(terms.at[d, h], arrived.at[d, h], send1.at[d, h], recv1.at[d, h], near_peers[d])
-
-    def second_copy(e, h):
-        return send(
-            partial.at[h], arrived_far.at[e, h], send2.at[e, h], recv2.at[e, h], far_peers[e]
-        )
-
-    def third_copy(d, h):
-        here = grid.at[near * h + low]
-        return send(here, here, send3.at[d, h], recv3.at[d, h], near_peers[d])
-
-    for h in range(far):
-        for d in range(1, near):
-            first_copy(d, h).start()
-
-    for load in loads[4:8]:
+    def first_copy(d):
+        return send(terms.at[d], arrived.at[d], send1.at[d], recv1.at[d], near_peers[d])
+
+    def second_copy(e):
+        return send(partial, arrived_far.at[e], send2.at[e], recv2.at[e], far_peers[e])
+
+    def third_copy(d):
+        return send(grid.at[low], grid.at[low], send3.at[d], recv3.at[d], near_peers[d])
+
+    for d in range(1, near):
+        first_copy(d).start()
+
+    for load in loads[2:6]:
         load.wait()
-    loads[2].wait()
     total_rows = n * rows
     for j in range(dest.shape[0]):
         cut = slice(j * 128, (j + 1) * 128)
-        wanted = dest[j : j + 1, :] * rows + grid_row[j : j + 1, :]
+        column = dest[j : j + 1, :]
+        column = column % near * far + column // near
+        wanted = column * rows + grid_row[j : j + 1, :]
         hot = (lax.broadcasted_iota(jnp.int32, (total_rows, 128), 0) == wanted).astype(jnp.float32)
         hot = hot.astype(jnp.bfloat16)
         one_hot[:total_rows, cut] = hot
@@ -154,32 +151,26 @@
         tap = jnp.maximum(1.0 - r * r, 0.0)
         weights[:, cut] = tap * tap
 
-    for h in range(far):
-        total = terms[0, h]
-        for d in range(1, near):
-            first_copy(d, h).wait_recv()
-            total = total + arrived[d, h]
-        partial[h] = total
-        for e in range(1, far):
-            second_copy(e, h).start()
-    for h in range(far):
-        total = partial[h]
-        for e in range(1, far):
-            second_copy(e, h).wait_recv()
-            total = total + arrived_far[e, h]
-        grid[pl.ds(near * h + low, 1)] = total[None]
-        for d in range(1, near):
-            third_copy(d, h).start()
-    stores = [pltpu.make_async_copy(grid.at[me], grid_out.at[0, 0], store_sem.at[0])]
-    stores[0].start()
-    for h in range(far):
-        for d in range(1, near):
-            first_copy(d, h).wait_send()
-        for e in range(1, far):
-            second_copy(e, h).wait_send()
-    for h in range(far):
-        for d in range(1, near):
-            third_copy(d, h).wait_recv()
+    total = terms[0]
+    for d in range(1, near):
+        first_copy(d).wait_recv()
+        total = total + arrived[d]
+    partial[...] = total
+    for e in range(1, far):
+        second_copy(e).start()
+    for e in range(1, far):
+        second_copy(e).wait_recv()
+        total = total + arrived_far[e]
+    grid[pl.ds(low, 1)] = total[None]
+    for d in range(1, near):
+        third_copy(d).start()
+    grid_out[0, 0] = grid[low, high]
+    for d in range(1, near):
+        first_copy(d).wait_send()
+    for e in range(1, far):
+        second_copy(e).wait_send()
+    for d in range(1, near):
+        third_copy(d).wait_recv()
 
     turned = grid[...].reshape(total_rows, 2 * M).T
     coarse = turned.astype(jnp.bfloat16)
@@ -197,13 +188,8 @@
         residual[0, 0:1, cut] = jnp.where(live, observed[0, 0:1, cut] - real_sum, 0.0)
         residual[0, 1:2, cut] = jnp.where(live, observed[0, 1:2, cut] - imag_sum, 0.0)
 
-    stores.append(pltpu.make_async_copy(residual, residual_out, store_sem.at[1]))
-    stores[1].start()
-    for h in range(far):
-        for d in range(1, near):
-            third_copy(d, h).wait_send()
-    for store in stores:
-        store.wait()
+    for d in range(1, near):
+        third_copy(d).wait_send()
 
 
 def body(
@@ -214,12 +200,14 @@
     rows, pixels = facets.shape[2], facets.shape[3]
     count = dest_column.shape[0]
     tall = (count // 128, 128)
+    vmem = pl.BlockSpec(memory_space=pltpu.VMEM)
+    smem = pl.BlockSpec(memory_space=pltpu.SMEM)
     hbm = pl.BlockSpec(memory_space=pltpu.HBM)
     f32, bf16 = jnp.float32, jnp.bfloat16
     arrays = (
         facet_offsets,
+        row_counts,
         subgrid_offsets,
-        row_counts,
         facets,
         dest_column.reshape(tall),
         grid_row.reshape(tall),
@@ -227,18 +215,18 @@
         observed,
         jnp.asarray(dft_constant(pixels)),
     )
-    spaces = [pltpu.SMEM] * 3 + [pltpu.VMEM] * 6
+    spaces = [pltpu.SMEM] + [pltpu.VMEM] * 6
     shapes = (
-        jax.ShapeDtypeStruct((1, 1, rows, 2 * M), f32),
-        jax.ShapeDtypeStruct(observed.shape, f32),
+        (1, 1, rows, 2 * M),
+        observed.shape,
     )
     return pl.pallas_call(
         functools.partial(kernel, n),
-        out_shape=shapes,
-        in_specs=[hbm] * len(arrays),
-        out_specs=(hbm, hbm),
+        out_shape=tuple(pltpu.VMEM(shape, f32) for shape in shapes),
+        in_specs=[smem if array.size == 1 else hbm for array in arrays],
+        out_specs=(vmem, vmem),
         scratch_shapes=[
-            *[space(array.shape, array.dtype) for space, array in zip(spaces, arrays)],
+            *[space(array.shape, array.dtype) for space, array in zip(spaces, arrays[2:])],
             pltpu.VMEM((n, pixels), f32),
             pltpu.VMEM((n, pixels), f32),
             pltpu.VMEM((2 * rows * n, pixels), bf16),
@@ -246,25 +234,26 @@
             pltpu.VMEM((n, M), f32),
             pltpu.VMEM((NEAR, far, rows, 2 * M), f32),
             pltpu.VMEM((NEAR, far, rows, 2 * M), f32),
-            pltpu.VMEM((n, rows, 2 * M), f32),
+            pltpu.VMEM((NEAR, far, rows, 2 * M), f32),
             pltpu.VMEM((2 * n * rows, count), bf16),
             pltpu.VMEM((M, count), f32),
             pltpu.VMEM((far, far, rows, 2 * M), f32),
             pltpu.VMEM((far, rows, 2 * M), f32),
-            pltpu.VMEM(observed.shape, f32),
-            pltpu.SemaphoreType.DMA((len(arrays),)),
-            pltpu.SemaphoreType.DMA((2,)),
-            pltpu.SemaphoreType.DMA((NEAR, far)),
-            pltpu.SemaphoreType.DMA((NEAR, far)),
-            pltpu.SemaphoreType.DMA((far, far)),
-            pltpu.SemaphoreType.DMA((far, far)),
-            pltpu.SemaphoreType.DMA((NEAR, far)),
-            pltpu.SemaphoreType.DMA((NEAR, far)),
+            pltpu.SemaphoreType.DMA((len(spaces),)),
+            pltpu.SemaphoreType.DMA((NEAR,)),
+            pltpu.SemaphoreType.DMA((NEAR,)),
+            pltpu.SemaphoreType.DMA((far,)),
+            pltpu.SemaphoreType.DMA((far,)),
+            pltpu.SemaphoreType.DMA((NEAR,)),
+            pltpu.SemaphoreType.DMA((NEAR,)),
         ],
         compiler_params=pltpu.CompilerParams(
-            collective_id=0, has_side_effects=True, vmem_limit_bytes=64 * 1024 * 1024
+            collective_id=0, has_side_effects=True, vmem_limit_bytes=40 * 1024 * 1024
         ),
-    )(*arrays)
+    )(*[
+        array if array.size == 1 else pltpu.with_memory_space_constraint(array, pltpu.HBM)
+        for array in arrays
+    ])
 
 
 def solution(mesh):

time: 23.8 us -> 21.5 us (0.903)
  local copies, waits for them, and re-layouts: 2.62 us -> 1.21 us
  Pallas kernels: 18.9 us -> 18.2 us
    unnamed x2, local copies, waits for them, and re-layouts: 2.62 us -> 1.21 us
    pallas_call x1, Pallas kernels: 18.9 us -> 18.2 us  [body(): pl.pallas_call(functools.partial(kernel, n), out_shape=tuple((pltpu.VMEM(...]
where the time goes in v3:
time: 21.5 us; the launch traced here: 21.3 us
  Pallas kernels  18.2 us (85%)
  between operations  1.93 us (9%)
  local copies, waits for them, and re-layouts  1.21 us (6%)
    pallas_call x1, Pallas kernels, body(): pl.pallas_call(functools.partial(kernel, n), out_shape=tuple((pltpu.VMEM(...  18.2 us
    unnamed x2, local copies, waits for them, and re-layouts  1.21 us

profile of v3, /device:TPU:0, one launch (start us, length us, event | category | flops | bytes accessed | tf_op | source)
XLA Modules:
  0.0 21.3 jit_solution(195465448247392809)
XLA Ops:
  1.9 18.2 %shard_map.104 = (f32[1,1,8,256]{3,2,1,0:T(8,128)S(1)}, f32[1,2,2048]{2,1,0:T(2,128)S(1)}) custom-call(s32[1]{0:T(128)S(6)} %copy.15.refs_0_, s32[1]{0:T(128)S(6)} %copy.16.refs_1_, s32[16]{0:T(128)} %refs_2_.1, f32[1,1,8,4096]{3,2,1,0:T(8,128)} %refs_3_.1, s32[16,128]{1,0:T(8,128)} %bitcast.3, s32[16,128]{1,0:T(8,128)} %bitcast.4, f32[16,128]{1,0:T(8,128)} %bitcast.5, ...), custom_call_target="tpu_custom_call" | custom-call | tf_op jit(solution)/shard_map/pallas_call | solution.py:223
  20.1 0.6 %copy.13 = f32[1,1,8,256]{3,2,1,0:T(8,128)} copy(f32[1,1,8,256]{3,2,1,0:T(8,128)S(1)} %get-tuple-element.2) | data formatting | bytes 16384
  20.7 0.6 %copy.14 = f32[1,2,2048]{2,1,0:T(2,128)} copy(f32[1,2,2048]{2,1,0:T(2,128)S(1)} %get-tuple-element.3) | data formatting | bytes 32768
